TPU v7x, 128 devices: a whole 4x4x4 slice. The times are simulated.
128 devices in a mesh: ia: 16 (over x, z), ja: 4 (over y), ka: 2 (over core).
Axes of the slice: x: 4, y: 4, z: 4, core: 2. Of those that a mesh axis runs over, the one named last changes fastest.
Arguments:
- tensor: float32 [1024, 1024, 512], P('ia', 'ja', 'ka'), may hold values from -6 to 6
- factor_first: float32 [1024, 32], P(('ia', 'ja', 'ka')), may hold values from -0.75 to 0.75
- factor_second: float32 [1024, 32], P(('ja', 'ia', 'ka')), may hold values from -0.375 to 0.375
- factor_third: float32 [512, 32], P(('ka', 'ia', 'ja')), may hold values from -0.375 to 0.375
Outputs:
- gradient: float32 [1024, 32], P(('ia', 'ja', 'ka'))
All inputs are finite; a program needn't handle non-finite values.
Results may differ from a plain program's by a relative error of at most 0.000082.
Values sent between devices are 32-bit elements; how exact they have to be, the bound alone decides.
No kernel may reach another device: no remote copies, remote signals or barrier semaphores. Data moves between devices by JAX's collectives and lax.ppermute only.
A program may use at most 64 MiB of HBM per device.

v0:
```python
import jax
import jax.numpy as jnp
from jax import lax
from jax.sharding import PartitionSpec as P


def on_device(tensor, factor_first, factor_second, factor_third):
    third_block = lax.all_gather(factor_third, ("ia", "ja"), axis=0, tiled=True)
    second_block = lax.all_gather(factor_second, ("ia", "ka"), axis=0, tiled=True)
    partial_value = jnp.einsum("ijk,kr->ijr", tensor, third_block, precision=lax.Precision.HIGHEST)
    term = jnp.einsum("ijr,jr->ir", partial_value, second_block, precision=lax.Precision.HIGHEST)
    local_second = jnp.dot(factor_second.T, factor_second, precision=lax.Precision.HIGHEST)
    local_third = jnp.dot(factor_third.T, factor_third, precision=lax.Precision.HIGHEST)
    gram_second, gram_third = lax.psum((local_second, local_third), ("ia", "ja", "ka"))
    product = lax.psum_scatter(term, ("ja", "ka"), scatter_dimension=0, tiled=True)
    return (
        jnp.dot(factor_first, gram_second * gram_third, precision=lax.Precision.HIGHEST) - product
    )


def solution(mesh):
    return jax.shard_map(
        on_device,
        mesh=mesh,
        in_specs=(
            P("ia", "ja", "ka"),
            P(("ia", "ja", "ka"), None),
            P(("ja", "ia", "ka"), None),
            P(("ka", "ia", "ja"), None),
        ),
        out_specs=P(("ia", "ja", "ka"), None),
        check_vma=False,
    )
```

profile of v0, /device:TPU:1, one launch (start us, length us, event | category | flops | bytes accessed | tf_op | source)
XLA Modules:
  0.0 311.8 jit_solution(3374264157790472618)
XLA Ops:
  0.0 0.0 copy-start
  0.0 0.0 copy-start.1
  0.0 1.0 fusion.2
  1.0 1.0 fusion.3
  2.0 69.1 %all-reduce.1 = (f32[32,32]{1,0:T(8,128)S(1)}, f32[32,32]{1,0:T(8,128)S(1)}) all-reduce(f32[32,32]{1,0:T(8,128)S(1)} %fusion.2, f32[32,32]{1,0:T(8,128)S(1)} %fusion.3), channel_id=1, replica_groups=mesh['ia'=16,'ja'=4,'ka'=2] {'ia','ja','ka'}, use_global_device_ids=true, to_apply=%region_0.0 | all-reduce | flops 2048 | bytes 16384 | tf_op jit(solution)/shard_map/psum | solution.py:14
  71.0 22.8 %all_gather.7 = f32[256,32]{1,0:T(8,128)S(1)} all-gather(f32[8,32]{1,0:T(8,128)} %param.6), channel_id=1, replica_groups=mesh['ia'=16,'ja'=4,'ka'=2] {'ia','ka'}, dimensions={0}, use_global_device_ids=true | all-gather | bytes 33792 | tf_op jit(solution)/shard_map/all_gather | solution.py:9
  93.8 0.1 copy.15
  93.9 146.5 %all-gather = f32[64,4,32]{2,1,0:T(4,128)S(1)} all-gather(f32[1,4,32]{2,1,0:T(4,128)} %bitcast.23), channel_id=1, replica_groups=mesh['ia'=16,'ja'=4,'ka'=2] {'ia','ja'}, dimensions={0}, use_global_device_ids=true | all-gather | bytes 33280 | tf_op jit(solution)/shard_map/all_gather | solution.py:8
  240.4 21.1 %multiply_reduce_fusion = f32[32,64]{0,1:T(8,128)S(1)} fusion(f32[64,256,256]{2,1,0:T(8,128)} %param.4, f32[256,32,1]{1,0,2:T(8,128)S(1)} %bitcast.20, f32[32,256]{1,0:T(8,128)S(1)} %copy.15), kind=kOutput, calls=%fused_computation | convolution fusion | flops 1611659264 | bytes 16850944 | tf_op jit(solution)/shard_map/ijk,kr->ijr/dot_general | solution.py:10
  261.6 48.3 %all-reduce = f32[64,32]{1,0:T(8,128)S(1)} all-reduce(f32[64,32]{1,0:T(8,128)S(1)} %bitcast.22), channel_id=2, replica_groups=mesh['ia'=16,'ja'=4,'ka'=2] {'ja','ka'}, use_global_device_ids=true, to_apply=%region_2.0.clone | all-reduce | flops 2048 | bytes 16384
  309.8 0.0 copy-done.1
  309.8 0.6 dynamic-slice
  311.1 0.0 copy-done
  311.1 0.7 fusion
Async XLA Ops:
  0.0 311.1 %copy-start = (f32[8,32]{1,0:T(8,128)S(1)}, f32[8,32]{1,0:T(8,128)}, u32[]{:S(2)}) copy-start(f32[8,32]{1,0:T(8,128)} %param.5) | copy-start | bytes 3076
  0.0 309.8 %copy-start.1 = (u32[128]{0:T(128)S(1)}, u32[128]{0:T(128)}, u32[]{:S(2)}) copy-start(u32[128]{0:T(128)} %constant.6) | copy-start | bytes 1540
where the time goes:
time: 314 us; the launch traced here: 312 us
  blocking collectives  287 us (91%)
  matrix products  23.8 us (8%)
    all_gather x1, blocking collectives, on_device(): third_block = lax.all_gather(factor_third, ('ia', 'ja'), axis=0, tiled=True)  147 us
    psum x1, blocking collectives, on_device(): lax.psum((local_second, local_third), ('ia', 'ja', 'ka'))  69.1 us
    unnamed x1, blocking collectives  48.3 us
    all_gather x1, blocking collectives, on_device(): lax.all_gather(factor_second, ('ia', 'ka'), axis=0, tiled=True)  22.8 us
    dot_general x1, matrix products, on_device(): jnp.einsum('ijk,kr->ijr', tensor, third_block, precision=lax.Precision.HI...  21.1 us

commit v1 on v0

v1 whole, which is shorter than its diff:
```python
import functools

import jax
import jax.numpy as jnp
from jax import lax
from jax.experimental import pallas as pl
from jax.experimental.pallas import tpu as pltpu
from jax.sharding import PartitionSpec as P

RANK = 32
EVERY = ("ia", "ja", "ka")
HIGHEST = lax.Precision.HIGHEST


def iota(shape, axis):
    return lax.broadcasted_iota(jnp.int32, shape, axis)


def split(value):
    high = value.astype(jnp.bfloat16)
    low = (value - high.astype(jnp.float32)).astype(jnp.bfloat16)
    return high, low


def mm(left, right):
    return jnp.dot(left, right, preferred_element_type=jnp.float32)


def unpacked(packed, rows, source, place):
    count, lanes = packed.shape
    pick = jnp.where(iota((rows, count), 1) == source, 1.0, 0.0).astype(jnp.bfloat16)
    keep = iota((rows, lanes), 1) // RANK == place
    parts = []
    for part in split(packed):
        parts.append(jnp.where(keep, mm(pick, part), 0.0).astype(jnp.bfloat16))
    return parts


def folding(lanes, columns, shift):
    row, column = iota((lanes, columns), 0), iota((lanes, columns), 1)
    hit = (column - shift == row % RANK) & (column >= shift) & (column < shift + RANK)
    return jnp.where(hit, 1.0, 0.0).astype(jnp.bfloat16)


def term_kernel(steps, tensor_ref, packed_ref, term_ref, weight_ref, second_ref, sums_ref):
    ja, ka = lax.axis_index("ja"), lax.axis_index("ka")
    rows, js, ks = tensor_ref.shape
    wide = 4 * RANK

    third_at = iota((ks, 1), 0)
    high, low = unpacked(packed_ref[:, 256:384], ks, third_at // 4 * 2 + ka, third_at % 4)
    weight = mm(high, folding(wide, wide, 0)) + mm(low, folding(wide, wide, RANK))
    weight_ref[...] = weight.astype(jnp.bfloat16)

    second_at = iota((js, 1), 0)
    high, low = unpacked(packed_ref[:, 0:256], js, second_at // 16 * 8 + 2 * ja + second_at // 8 % 2, second_at % 8)
    both = folding(2 * wide, wide, 0) + folding(2 * wide, wide, RANK)
    second_ref[...] = mm(high, both) + mm(low, both)

    per = rows // steps

    def step(at, carry):
        block = tensor_ref[pl.ds(at * per, per)].reshape(per * js, ks)
        high, low = split(block)
        partial = mm(high, weight_ref[...]) + mm(low, weight_ref[...])
        scaled = partial.reshape(per, js, wide) * second_ref[...][None]
        sums_ref[pl.ds(at * per, per)] = jnp.sum(scaled.reshape(per, js // 8, 8, wide), axis=1)
        return carry

    lax.fori_loop(0, steps, step, 0)
    total = jnp.sum(sums_ref[...], axis=1)
    term_ref[...] = total[:, 0:RANK] + total[:, RANK : 2 * RANK]


def gradient_kernel(packed_ref, first_ref, terms_ref, gradient_ref):
    def gram(block):
        lanes = block.shape[1]
        whole = lax.dot_general(block, block, (((0,), (0,)), ((), ())), precision=HIGHEST)
        kept = jnp.where(iota((lanes, lanes), 0) // RANK == iota((lanes, lanes), 1) // RANK, whole, 0.0)
        fold = jnp.where(iota((lanes, RANK), 0) % RANK == iota((lanes, RANK), 1), 1.0, 0.0)
        tall = jnp.dot(kept, fold, precision=HIGHEST)
        return jnp.sum(tall.reshape(lanes // RANK, RANK, RANK), axis=0)

    both = gram(packed_ref[:, 0:256]) * gram(packed_ref[:, 256:384])
    rows = first_ref.shape[0]
    product = jnp.sum(terms_ref[...].reshape(-1, rows, RANK), axis=0)
    gradient_ref[...] = jnp.dot(first_ref[...], both, precision=HIGHEST) - product


def on_device(tensor, first, second, third):
    rows, js, ks = tensor.shape
    own = jnp.concatenate([second.reshape(1, 256), third.reshape(1, 128)], axis=1)
    packed = lax.all_to_all(jnp.broadcast_to(own, (128, 384)), EVERY, 0, 0, tiled=True)
    tensor = pltpu.with_memory_space_constraint(tensor, pltpu.VMEM)
    term = pl.pallas_call(
        functools.partial(term_kernel, 16),
        out_shape=jax.ShapeDtypeStruct((rows, RANK), jnp.float32),
        in_specs=[pl.BlockSpec(memory_space=pltpu.VMEM)] * 2,
        out_specs=pl.BlockSpec(memory_space=pltpu.VMEM),
        scratch_shapes=[
            pltpu.VMEM((ks, 4 * RANK), jnp.bfloat16),
            pltpu.VMEM((js, 4 * RANK), jnp.float32),
            pltpu.VMEM((rows, 8, 4 * RANK), jnp.float32),
        ],
        compiler_params=pltpu.CompilerParams(vmem_limit_bytes=24 * 1024 * 1024),
        cost_estimate=pl.CostEstimate(flops=2 * rows * js * ks * 512, bytes_accessed=rows * js * ks * 4, transcendentals=0),
        name="term",
    )(tensor, packed)
    terms = lax.all_to_all(term, ("ja", "ka"), 0, 0, tiled=True)
    return pl.pallas_call(
        gradient_kernel,
        out_shape=jax.ShapeDtypeStruct(first.shape, jnp.float32),
        in_specs=[pl.BlockSpec(memory_space=pltpu.VMEM)] * 3,
        out_specs=pl.BlockSpec(memory_space=pltpu.VMEM),
        compiler_params=pltpu.CompilerParams(vmem_limit_bytes=16 * 1024 * 1024),
        name="gradient",
    )(packed, first, terms)


def solution(mesh):
    return jax.shard_map(
        on_device,
        mesh=mesh,
        in_specs=(
            P("ia", "ja", "ka"),
            P(("ia", "ja", "ka"), None),
            P(("ja", "ia", "ka"), None),
            P(("ka", "ia", "ja"), None),
        ),
        out_specs=P(("ia", "ja", "ka"), None),
        check_vma=False,
    )
```

time: 314 us -> 48.4 us (0.15)
  blocking collectives: 287 us -> 29.4 us
  matrix products: 23.8 us -> 0 us
  Pallas kernels: 0 us -> 9.88 us
  local copies, waits for them, and re-layouts: 0.65 us -> 8.09 us
    all_gather x2 -> x0, blocking collectives: 169 us -> none  [the longest x1 147 us: on_device(): third_block = lax.all_gather(factor_third, ('ia', 'ja'), axis=0, tiled=True)]
    psum x1 -> x0, blocking collectives: 69.1 us -> none  [on_device(): lax.psum((local_second, local_third), ('ia', 'ja', 'ka'))]
    unnamed x1 -> x0, blocking collectives: 48.3 us -> none
    all_to_all x0 -> x2, blocking collectives: none -> 29.4 us  [the longest x1 21.7 us: on_device(): lax.all_to_all(jnp.broadcast_to(own, (128, 384)), EVERY, 0, 0, tiled=True)]
    dot_general x4 -> x0, matrix products: 23.8 us -> none  [the longest x1 21.1 us: on_device(): jnp.einsum('ijk,kr->ijr', tensor, third_block, precision=lax.Precision.HI...]
    pallas_call x0 -> x2, Pallas kernels: none -> 9.88 us  [the longest x1 7.98 us: on_device(): pl.pallas_call(functools.partial(term_kernel, 16), out_shape=jax.ShapeDty...]
    unnamed x6 -> x7, local copies, waits for them, and re-layouts: 0.65 us -> 5.94 us
where the time goes in v1:
time: 48.4 us; the launch traced here: 48.1 us
  blocking collectives  29.4 us (61%)
  Pallas kernels  9.88 us (20%)
  local copies, waits for them, and re-layouts  8.09 us (17%)
  other arithmetic  0.69 us (1%)
    all_to_all x1, blocking collectives, on_device(): lax.all_to_all(jnp.broadcast_to(own, (128, 384)), EVERY, 0, 0, tiled=True)  21.7 us
    pallas_call x1, Pallas kernels, on_device(): pl.pallas_call(functools.partial(term_kernel, 16), out_shape=jax.ShapeDty...  7.98 us
    all_to_all x1, blocking collectives, on_device(): terms = lax.all_to_all(term, ('ja', 'ka'), 0, 0, tiled=True)  7.67 us
    unnamed x7, local copies, waits for them, and re-layouts  5.94 us
    pallas_call x1, Pallas kernels, on_device(): pl.pallas_call(gradient_kernel, out_shape=jax.ShapeDtypeStruct(first.shap...  1.9 us

profile of v1, /device:TPU:1, one launch (start us, length us, event | category | flops | bytes accessed | tf_op | source)
XLA Modules:
  0.0 48.1 jit_solution(3423415666031445206)
XLA Ops:
  0.0 0.0 copy-start.1
  0.0 0.8 %reshape.14 = f32[1,256]{1,0:T(1,128)S(1)} reshape(f32[8,32]{1,0:T(8,128)} %param.6) | data formatting | bytes 2048 | tf_op jit(solution)/shard_map/reshape | solution.py:92
  0.8 0.8 %reshape.15 = f32[1,128]{1,0:T(1,128)S(1)} reshape(f32[4,32]{1,0:T(4,128)} %param.7) | data formatting | bytes 1024 | tf_op jit(solution)/shard_map/reshape | solution.py:92
  1.6 0.1 broadcast_in_dim.2
  1.7 21.7 %all_to_all.19 = f32[128,1,384]{2,1,0:T(1,128)S(1)} all-to-all(f32[128,1,384]{2,1,0:T(1,128)S(1)} %broadcast_in_dim.2), channel_id=1, replica_groups=mesh['ia'=16,'ja'=4,'ka'=2] {'ia','ja','ka'}, dimensions={0} | all-to-all | bytes 393216 | tf_op jit(solution)/shard_map/all_to_all | solution.py:93
  23.4 0.0 copy-start
  23.4 5.8 %copy-done = f32[64,256,256]{2,1,0:T(8,128)S(1)} copy-done((f32[64,256,256]{2,1,0:T(8,128)S(1)}, f32[64,256,256]{2,1,0:T(8,128)}, u32[]{:S(2)}) %copy-start) | copy-done | bytes 16777240
  29.2 8.0 %term.1 = f32[64,32]{1,0:T(8,128)S(1)} custom-call(f32[64,256,256]{2,1,0:T(8,128)S(1)} %copy-done, f32[128,384]{1,0:T(8,128)S(1)} %bitcast.5), custom_call_target="tpu_custom_call" | custom-call | flops 4294967296 | bytes 16777216 | tf_op jit(solution)/shard_map/term/pallas_call | solution.py:95
  37.2 0.1 reshape.17
  37.3 7.7 %all_to_all.20 = f32[8,1,256]{2,1,0:T(1,128)S(1)} all-to-all(f32[8,1,256]{2,1,0:T(1,128)S(1)} %reshape.17), channel_id=1, replica_groups=mesh['ia'=16,'ja'=4,'ka'=2] {'ja','ka'}, dimensions={0} | all-to-all | bytes 16384 | tf_op jit(solution)/shard_map/all_to_all | solution.py:109
  44.9 0.5 %broadcast.5 = f32[]{:T(128)} broadcast(f32[]{:T(128)} %constant.7), dimensions={} | broadcast | bytes 8 | tf_op jit(solution)/shard_map/all_to_all | solution.py:109
  45.4 0.7 %reduce.2 = f32[8,256]{1,0:T(8,128)S(1)} reduce(f32[8,1,256]{2,1,0:T(1,128)S(1)} %all_to_all.20, f32[]{:T(128)} %broadcast.5), dimensions={1}, to_apply=%all_to_all.15.reduce_sub_computation | reduce | bytes 16388 | tf_op jit(solution)/shard_map/all_to_all | solution.py:109
  46.1 0.1 reshape.18
  46.2 0.0 copy-done.1
  46.2 1.9 %gradient.1 = f32[8,32]{1,0:T(8,128)} custom-call(f32[128,384]{1,0:T(8,128)S(1)} %bitcast.6, f32[8,32]{1,0:T(8,128)S(1)} %copy-done.1, f32[64,32]{1,0:T(8,128)S(1)} %bitcast.8), custom_call_target="tpu_custom_call" | custom-call | tf_op jit(solution)/shard_map/gradient/pallas_call | solution.py:110
  (2 shorter events, 0.0 us)
Async XLA Ops:
  0.0 46.2 %copy-start.1 = (f32[8,32]{1,0:T(8,128)S(1)}, f32[8,32]{1,0:T(8,128)}, u32[]{:S(2)}) copy-start(f32[8,32]{1,0:T(8,128)} %first_ref.1) | copy-start | bytes 3076
  23.4 5.8 %copy-start = (f32[64,256,256]{2,1,0:T(8,128)S(1)}, f32[64,256,256]{2,1,0:T(8,128)}, u32[]{:S(2)}) copy-start(f32[64,256,256]{2,1,0:T(8,128)} %tensor_ref.1) | copy-start | bytes 50331652

commit v2 on v0

v2 whole, which is shorter than its diff:
```python
import functools

import jax
import jax.numpy as jnp
from jax import lax
from jax.experimental import pallas as pl
from jax.experimental.pallas import tpu as pltpu
from jax.sharding import PartitionSpec as P

RANK = 32
EVERY = ("ia", "ja", "ka")
CHUNK = 4
CHUNKS = 16
GROUP = 4
AHEAD = 8
PER_HOP = 2
HIGHEST = lax.Precision.HIGHEST


def iota(shape, axis):
    return lax.broadcasted_iota(jnp.int32, shape, axis)


def split(value):
    high = value.astype(jnp.bfloat16)
    low = (value - high.astype(jnp.float32)).astype(jnp.bfloat16)
    return high, low


def chunks_ahead():
    ia, ja = lax.axis_index("ia"), lax.axis_index("ja")
    hops = sum(jnp.minimum(at, 4 - at) for at in (ia // 4, ia % 4, ja))
    return jnp.clip(AHEAD - PER_HOP * hops, 0, CHUNKS)


def chunk_copy(tensor_hbm, tensor_ref, sem, at):
    here = pl.ds(at * CHUNK, CHUNK)
    return pltpu.make_async_copy(tensor_hbm.at[here], tensor_ref.at[here], sem)


def own_kernel(second_hbm, third_hbm, tensor_hbm, own_ref, tensor_ref, second_ref, third_ref, sems):
    second_copy = pltpu.make_async_copy(second_hbm, second_ref, sems.at[0])
    third_copy = pltpu.make_async_copy(third_hbm, third_ref, sems.at[1])
    second_copy.start()
    third_copy.start()
    ahead = chunks_ahead()

    @pl.loop(0, ahead)
    def begin(at):
        chunk_copy(tensor_hbm, tensor_ref, sems.at[2 + at], at).start()

    def row(value):
        count = value.shape[0]
        lanes = count * RANK
        spread = jnp.where(iota((RANK, lanes), 0) == iota((RANK, lanes), 1) % RANK, 1.0, 0.0)
        wide = jnp.dot(value, spread, precision=HIGHEST)
        kept = jnp.where(iota((count, lanes), 1) // RANK == iota((count, lanes), 0), wide, 0.0)
        return jnp.sum(kept, axis=0, keepdims=True)

    second_copy.wait()
    third_copy.wait()
    own = jnp.concatenate([row(second_ref[...]), row(third_ref[...])], axis=1)
    own_ref[...] = jnp.broadcast_to(own[None], own_ref.shape)

    @pl.loop(0, ahead)
    def end(at):
        chunk_copy(tensor_hbm, tensor_ref, sems.at[2 + at], at).wait()


def term_kernel(tensor_hbm, packed_ref, held_ref, term_ref, tensor_ref, third_ref, second_ref, sums_ref, sems):
    del held_ref
    ahead = chunks_ahead()

    @pl.loop(ahead, CHUNKS)
    def begin(at):
        chunk_copy(tensor_hbm, tensor_ref, sems.at[at], at).start()

    def arrive(at):
        @pl.when(at >= ahead)
        def wait():
            chunk_copy(tensor_hbm, tensor_ref, sems.at[at], at).wait()

    rows, js, ks = tensor_ref.shape
    wide = 4 * RANK
    ja, ka = lax.axis_index("ja"), lax.axis_index("ka")

    def spread(source, into, start, stride):
        count = source.shape[0]
        for part in range(4):
            turned = pltpu.roll(source, (wide - RANK * part) % wide, 1)
            into[pl.ds(start + part, count, stride=stride), :] = turned

    spread(packed_ref[pl.ds(3 * ka + 2, ks // 4, stride=6), :], third_ref, 0, 4)
    for core in range(2):
        for half in range(2):
            source = packed_ref[pl.ds(6 * ja + 3 * core + half, js // 16, stride=24), :]
            spread(source, second_ref, 8 * core + 4 * half, 16)
    lane = iota((ks, wide), 1)
    high, low = split(third_ref[...])
    turned = pltpu.roll(low.astype(jnp.float32), RANK, 1)
    weight = jnp.where(lane < RANK, high.astype(jnp.float32), jnp.where(lane < 2 * RANK, turned, 0.0)).astype(jnp.bfloat16)
    weight = jnp.concatenate([weight, jnp.zeros_like(weight)], axis=1)
    second = second_ref[...]
    second_ref[...] = jnp.where(lane < RANK, second, pltpu.roll(second, RANK, 1))

    def contract(*sums):
        for unit in range(2):
            pltpu.matmul_push_rhs(weight, 0, unit)
        for unit in range(2):
            pltpu.matmul_acc_lhs(sums[unit], jnp.zeros((js, ks), jnp.bfloat16), load_staged_rhs=0)
            pltpu.matmul_pop(sums[unit])
        lag = len(sums) - 1

        def push(at, turn):
            high, low = split(tensor_ref[at])
            pltpu.matmul_acc_lhs(sums[turn % len(sums)], high)
            pltpu.matmul_acc_lhs(sums[turn % len(sums)], low)

        def pop(at, turn):
            scaled = pltpu.matmul_pop(sums[turn % len(sums)])[:, 0:wide] * second_ref[...]
            sums_ref[at] = jnp.sum(scaled.reshape(js // 8, 8, wide), axis=0)

        arrive(0)
        for step in range(lag):
            push(step, step)

        per = GROUP // CHUNK

        @pl.loop(0, rows // GROUP - 1)
        def block(group):
            for chunk in range(per):
                arrive(group * per + 1 + chunk)
            for step in range(GROUP):
                push(group * GROUP + lag + step, lag + step)
                pop(group * GROUP + step, step)

        for chunk in range(CHUNKS - per + 1, CHUNKS):
            arrive(chunk)
        for at in range(rows - GROUP, rows):
            if at + lag < rows:
                push(at + lag, at + lag)
            pop(at, at)

    pl.run_scoped(contract, *[pltpu.ACC(at % 2)((js, 256), jnp.float32) for at in range(4)])
    term_ref[...] = jnp.sum(sums_ref[...], axis=1).reshape(term_ref.shape)


def gram_kernel(packed_ref, first_ref, gram_ref):
    packed = packed_ref[...].reshape(128, 384)

    def gram(block):
        lanes = block.shape[1]
        whole = lax.dot_general(block, block, (((0,), (0,)), ((), ())), precision=HIGHEST)
        kept = jnp.where(iota((lanes, lanes), 0) // RANK == iota((lanes, lanes), 1) // RANK, whole, 0.0)
        fold = jnp.where(iota((lanes, RANK), 0) % RANK == iota((lanes, RANK), 1), 1.0, 0.0)
        tall = jnp.dot(kept, fold, precision=HIGHEST)
        return jnp.sum(tall.reshape(lanes // RANK, RANK, RANK), axis=0)

    both = gram(packed[:, 0:256]) * gram(packed[:, 256:384])
    gram_ref[...] = jnp.dot(first_ref[...], both, precision=HIGHEST)


def gradient_kernel(gram_ref, terms_ref, gradient_ref):
    total = jnp.sum(terms_ref[...], axis=0)
    gradient_ref[...] = gram_ref[...] - (total[:, 0:RANK] + total[:, RANK : 2 * RANK])


def fixed(value):
    return pltpu.with_memory_space_constraint(value, pltpu.VMEM)


def inhbm(value):
    return pltpu.with_memory_space_constraint(value, pltpu.HBM)


VMEM = pl.BlockSpec(memory_space=pltpu.VMEM)


def on_device(tensor, first, second, third):
    rows, js, ks = tensor.shape
    tensor = inhbm(tensor)
    own, held = pl.pallas_call(
        own_kernel,
        out_shape=(jax.ShapeDtypeStruct((128, 1, 384), jnp.float32), jax.ShapeDtypeStruct(tensor.shape, jnp.float32)),
        in_specs=[pl.BlockSpec(memory_space=pltpu.HBM)] * 3,
        out_specs=(VMEM, VMEM),
        scratch_shapes=[pltpu.VMEM((8, RANK), jnp.float32), pltpu.VMEM((4, RANK), jnp.float32), pltpu.SemaphoreType.DMA((2 + CHUNKS,))],
        compiler_params=pltpu.CompilerParams(vmem_limit_bytes=24 * 1024 * 1024),
        name="own",
    )(inhbm(second), inhbm(third), tensor)
    packed = lax.all_to_all(own, EVERY, 0, 0, tiled=True)
    term, _ = pl.pallas_call(
        term_kernel,
        out_shape=(jax.ShapeDtypeStruct((8, 8, 4 * RANK), jnp.float32), jax.ShapeDtypeStruct(tensor.shape, jnp.float32)),
        in_specs=[pl.BlockSpec(memory_space=pltpu.HBM), VMEM, VMEM],
        out_specs=(VMEM, VMEM),
        input_output_aliases={2: 1},
        scratch_shapes=[
            pltpu.VMEM((ks, 4 * RANK), jnp.float32),
            pltpu.VMEM((js, 4 * RANK), jnp.float32),
            pltpu.VMEM((rows, 8, 4 * RANK), jnp.float32),
            pltpu.SemaphoreType.DMA((CHUNKS,)),
        ],
        compiler_params=pltpu.CompilerParams(vmem_limit_bytes=24 * 1024 * 1024),
        cost_estimate=pl.CostEstimate(flops=2 * rows * js * ks * 512, bytes_accessed=rows * js * ks * 4, transcendentals=0),
        name="term",
    )(tensor, packed.reshape(384, 128), held)
    terms = lax.all_to_all(term, ("ja", "ka"), 0, 0, tiled=True)
    gram = pl.pallas_call(
        gram_kernel,
        out_shape=jax.ShapeDtypeStruct(first.shape, jnp.float32),
        in_specs=[VMEM] * 2,
        out_specs=VMEM,
        compiler_params=pltpu.CompilerParams(vmem_limit_bytes=16 * 1024 * 1024),
        cost_estimate=pl.CostEstimate(flops=1 << 27, bytes_accessed=1 << 20, transcendentals=0),
        name="gram",
    )(packed, first)
    return pl.pallas_call(
        gradient_kernel,
        out_shape=jax.ShapeDtypeStruct(first.shape, jnp.float32),
        in_specs=[VMEM] * 2,
        out_specs=VMEM,
        compiler_params=pltpu.CompilerParams(vmem_limit_bytes=4 * 1024 * 1024),
        name="gradient",
    )(gram, terms)


def solution(mesh):
    return jax.shard_map(
        on_device,
        mesh=mesh,
        in_specs=(
            P("ia", "ja", "ka"),
            P(("ia", "ja", "ka"), None),
            P(("ja", "ia", "ka"), None),
            P(("ka", "ia", "ja"), None),
        ),
        out_specs=P(("ia", "ja", "ka"), None),
        check_vma=False,
    )
```

time: 314 us -> 38.6 us (0.12)
  blocking collectives: 287 us -> 19.4 us
  matrix products: 23.8 us -> 0 us
  Pallas kernels: 0 us -> 11.6 us
  starting transfers between devices: 0 us -> 3.95 us
  waiting for transfers between devices: 0 us -> 3.46 us
    all_gather x2 -> x0, blocking collectives: 169 us -> none  [the longest x1 147 us: on_device(): third_block = lax.all_gather(factor_third, ('ia', 'ja'), axis=0, tiled=True)]
    psum x1 -> x0, blocking collectives: 69.1 us -> none  [on_device(): lax.psum((local_second, local_third), ('ia', 'ja', 'ka'))]
    unnamed x1 -> x0, blocking collectives: 48.3 us -> none
    dot_general x4 -> x0, matrix products: 23.8 us -> none  [the longest x1 21.1 us: on_device(): jnp.einsum('ijk,kr->ijr', tensor, third_block, precision=lax.Precision.HI...]
    all_to_all x0 -> x1, blocking collectives: none -> 19.4 us  [on_device(): packed = lax.all_to_all(own, EVERY, 0, 0, tiled=True)]
    pallas_call x0 -> x4, Pallas kernels: none -> 11.6 us  [the longest x1 6.02 us: on_device(): pl.pallas_call(term_kernel, out_shape=(jax.ShapeDtypeStruct((8, 8, 4 * RA...]
    all_to_all x0 -> x1, starting transfers between devices: none -> 3.95 us  [on_device(): terms = lax.all_to_all(term, ('ja', 'ka'), 0, 0, tiled=True)]
    all_to_all x0 -> x1, waiting for transfers between devices: none -> 3.46 us  [on_device(): terms = lax.all_to_all(term, ('ja', 'ka'), 0, 0, tiled=True)]
  transfers between devices with their start and end apart: 0 -> 1, of which waited for: 0 -> 1; matrix products, arithmetic and copies ran while one was open for 0% -> 0% of each run, Pallas kernels for 0% -> 3%
where the time goes in v2:
time: 38.6 us; the launch traced here: 38.4 us
  blocking collectives  19.4 us (50%)
  Pallas kernels  11.6 us (30%)
  starting transfers between devices  3.95 us (10%)
  waiting for transfers between devices  3.46 us (9%)
    all_to_all x1, blocking collectives, on_device(): packed = lax.all_to_all(own, EVERY, 0, 0, tiled=True)  19.4 us
    pallas_call x1, Pallas kernels, on_device(): pl.pallas_call(term_kernel, out_shape=(jax.ShapeDtypeStruct((8, 8, 4 * RA...  6.02 us
    all_to_all x1, starting transfers between devices, on_device(): terms = lax.all_to_all(term, ('ja', 'ka'), 0, 0, tiled=True)  3.95 us
    pallas_call x1, Pallas kernels, on_device(): pl.pallas_call(own_kernel, out_shape=(jax.ShapeDtypeStruct((128, 1, 384),...  3.59 us
    all_to_all x1, waiting for transfers between devices, on_device(): terms = lax.all_to_all(term, ('ja', 'ka'), 0, 0, tiled=True)  3.46 us
    pallas_call x1, Pallas kernels, on_device(): pl.pallas_call(gram_kernel, out_shape=jax.ShapeDtypeStruct(first.shape, j...  1.27 us
  transfers between devices with their start and end apart: 1, of which 1 were waited for; matrix products, arithmetic and copies ran while one was open for 0% of the time, Pallas kernels for 3%

profile of v2, /device:TPU:1, one launch (start us, length us, event | category | flops | bytes accessed | tf_op | source)
XLA Modules:
  0.0 38.4 jit_solution(1577960088349502431)
XLA Ops:
  0.0 3.6 %own.1 = (f32[128,1,384]{2,1,0:T(1,128)S(1)}, f32[64,256,256]{2,1,0:T(8,128)S(1)}) custom-call(f32[8,32]{1,0:T(8,128)} %second_hbm.1, f32[4,32]{1,0:T(4,128)} %third_hbm.1, f32[64,256,256]{2,1,0:T(8,128)} %tensor_hbm.3), custom_call_target="tpu_custom_call" | custom-call | tf_op jit(solution)/shard_map/own/pallas_call | solution.py:182
  3.6 19.4 %all_to_all.10.packed_ref = f32[128,1,384]{2,1,0:T(1,128)S(1)} all-to-all(f32[128,1,384]{2,1,0:T(1,128)S(1)} %get-tuple-element.8), channel_id=1, replica_groups=mesh['ia'=16,'ja'=4,'ka'=2] {'ia','ja','ka'}, dimensions={0} | all-to-all | bytes 393216 | tf_op jit(solution)/shard_map/all_to_all | solution.py:191
  23.0 0.0 copy-start
  23.0 6.0 %term.1 = (f32[8,8,128]{2,1,0:T(8,128)}, f32[64,256,256]{2,1,0:T(8,128)S(1)}) custom-call(f32[64,256,256]{2,1,0:T(8,128)} %tensor_hbm.3, f32[384,128]{1,0:T(8,128)S(1)} %bitcast.1, f32[64,256,256]{2,1,0:T(8,128)S(1)} %get-tuple-element.9.held_ref), custom_call_target="tpu_custom_call", output_to_operand_aliasing={{1}: (2, {})} | custom-call | flops 4294967296 | bytes 16777216 | tf_op jit(solution)/shard_map/term/pallas_call | solution.py:192
  29.0 4.0 %all-to-all-start.1 = ((f32[8,8,128]{2,1,0:T(8,128)}), f32[8,8,128]{2,1,0:T(8,128)S(1)}, u32[]{:S(2)}, u32[]{:S(2)}) async-start(f32[8,8,128]{2,1,0:T(8,128)} %get-tuple-element.10), calls=%async_computation.1 | async-start | bytes 65536 | tf_op jit(solution)/shard_map/all_to_all | solution.py:208
  33.0 0.0 copy-done
  33.0 1.3 %gram.1.gram_ref = f32[8,32]{1,0:T(8,128)S(1)} custom-call(f32[128,1,384]{2,1,0:T(1,128)S(1)} %all_to_all.10.packed_ref, f32[8,32]{1,0:T(8,128)S(1)} %copy-done), custom_call_target="tpu_custom_call" | custom-call | flops 134217728 | bytes 1048576 | tf_op jit(solution)/shard_map/gram/pallas_call | solution.py:209
  34.3 3.5 %all-to-all-done.1.terms_ref = f32[8,8,128]{2,1,0:T(8,128)S(1)} async-done(((f32[8,8,128]{2,1,0:T(8,128)}), f32[8,8,128]{2,1,0:T(8,128)S(1)}, u32[]{:S(2)}, u32[]{:S(2)}) %all-to-all-start.1) | async-done | bytes 32800 | tf_op jit(solution)/shard_map/all_to_all | solution.py:208
  37.7 0.7 %gradient.1 = f32[8,32]{1,0:T(8,128)} custom-call(f32[8,32]{1,0:T(8,128)S(1)} %gram.1.gram_ref, f32[8,8,128]{2,1,0:T(8,128)S(1)} %all-to-all-done.1.terms_ref), custom_call_target="tpu_custom_call" | custom-call | tf_op jit(solution)/shard_map/gradient/pallas_call | solution.py:218
Async XLA Ops:
  23.0 10.0 %copy-start = (f32[8,32]{1,0:T(8,128)S(1)}, f32[8,32]{1,0:T(8,128)}, u32[]{:S(2)}) copy-start(f32[8,32]{1,0:T(8,128)} %first_ref.1) | copy-start | bytes 3076
  29.0 8.7 %all-to-all-start.1 = ((f32[8,8,128]{2,1,0:T(8,128)}), f32[8,8,128]{2,1,0:T(8,128)S(1)}, u32[]{:S(2)}, u32[]{:S(2)}) async-start(f32[8,8,128]{2,1,0:T(8,128)} %get-tuple-element.10), calls=%async_computation.1 | async-start | bytes 65536 | tf_op jit(solution)/shard_map/all_to_all | solution.py:208

commit v3 on v2

v3 whole, which is shorter than its diff:
```python
import functools

import jax
import jax.numpy as jnp
from jax import lax
from jax.experimental import pallas as pl
from jax.experimental.pallas import tpu as pltpu
from jax.sharding import PartitionSpec as P

RANK = 32
EVERY = ("ia", "ja", "ka")
CHUNK = 4
CHUNKS = 16
GROUP = 8
AHEAD = 12
PER_HOP = 6
PER_ROW = 0
HIGHEST = lax.Precision.HIGHEST


def iota(shape, axis):
    return lax.broadcasted_iota(jnp.int32, shape, axis)


def split(value):
    high = value.astype(jnp.bfloat16)
    low = (value - high.astype(jnp.float32)).astype(jnp.bfloat16)
    return high, low


def chunks_ahead():
    ia, ja = lax.axis_index("ia"), lax.axis_index("ja")
    near = sum(jnp.minimum(at, 4 - at) for at in (ia // 4, ia % 4))
    return jnp.clip(AHEAD - PER_HOP * near - PER_ROW * jnp.minimum(ja, 4 - ja), 0, CHUNKS)


def chunk_copy(tensor_hbm, tensor_ref, sem, at):
    here = pl.ds(at * CHUNK, CHUNK)
    return pltpu.make_async_copy(tensor_hbm.at[here], tensor_ref.at[here], sem)


def own_kernel(second_hbm, third_hbm, tensor_hbm, own_ref, tensor_ref, second_ref, third_ref, sems):
    second_copy = pltpu.make_async_copy(second_hbm, second_ref, sems.at[0])
    third_copy = pltpu.make_async_copy(third_hbm, third_ref, sems.at[1])
    second_copy.start()
    third_copy.start()
    ahead = chunks_ahead()

    @pl.loop(0, ahead)
    def begin(at):
        chunk_copy(tensor_hbm, tensor_ref, sems.at[2 + at], at).start()

    def row(value):
        count = value.shape[0]
        lanes = count * RANK
        spread = jnp.where(iota((RANK, lanes), 0) == iota((RANK, lanes), 1) % RANK, 1.0, 0.0)
        wide = jnp.dot(value, spread, precision=HIGHEST)
        kept = jnp.where(iota((count, lanes), 1) // RANK == iota((count, lanes), 0), wide, 0.0)
        return jnp.sum(kept, axis=0, keepdims=True)

    second_copy.wait()
    third_copy.wait()
    own = jnp.concatenate([row(second_ref[...]), row(third_ref[...])], axis=1)
    own_ref[...] = jnp.broadcast_to(own[None], own_ref.shape)

    @pl.loop(0, ahead)
    def end(at):
        chunk_copy(tensor_hbm, tensor_ref, sems.at[2 + at], at).wait()


def term_kernel(tensor_hbm, packed_ref, held_ref, term_ref, tensor_ref, third_ref, second_ref, lines_ref, sums_ref, sems):
    del held_ref
    ahead = chunks_ahead()

    @pl.loop(ahead, CHUNKS)
    def begin(at):
        chunk_copy(tensor_hbm, tensor_ref, sems.at[at], at).start()

    def arrive(at):
        @pl.when(at >= ahead)
        def wait():
            chunk_copy(tensor_hbm, tensor_ref, sems.at[at], at).wait()

    rows, js, ks = tensor_ref.shape
    wide = 4 * RANK
    ja, ka = lax.axis_index("ja"), lax.axis_index("ka")

    def spread(source, into, start, stride):
        count = source.shape[0]
        for part in range(4):
            turned = pltpu.roll(source, (wide - RANK * part) % wide, 1)
            into[pl.ds(start + part, count, stride=stride), :] = turned

    spread(packed_ref[pl.ds(3 * ka + 2, ks // 4, stride=6), :], third_ref, 0, 4)
    for core in range(2):
        for half in range(2):
            source = packed_ref[pl.ds(6 * ja + 3 * core + half, js // 16, stride=24), :]
            spread(source, second_ref, 8 * core + 4 * half, 16)
    both = jnp.where(iota((js, wide), 1) < RANK, second_ref[...], pltpu.roll(third_ref[...], RANK, 1)).T
    high, low = split(both[0:RANK])
    left = jnp.concatenate([high, low], axis=0)
    lines_ref[...] = jnp.concatenate([both[RANK : 2 * RANK]] * 2, axis=0)

    def contract(*sums):
        lag = len(sums) - 1

        def push(at, turn):
            into = sums[turn % len(sums)]
            for register, part in enumerate(split(tensor_ref[at])):
                pltpu.matmul_push_rhs(part, register, turn % 2)
                pltpu.matmul_acc_lhs(into, left, load_staged_rhs=register)

        def pop(at, turn):
            scaled = pltpu.matmul_pop(sums[turn % len(sums)]) * lines_ref[...]
            scaled = scaled[:, 0:wide] + scaled[:, wide : 2 * wide]
            sums_ref[at] = scaled[0:RANK] + scaled[RANK : 2 * RANK]

        arrive(0)
        for step in range(lag):
            push(step, step)

        per = GROUP // CHUNK
        free = jnp.minimum(jnp.maximum(ahead - 1, 0) // per, rows // GROUP - 1)

        def contract_group(group):
            for step in range(GROUP):
                push(group * GROUP + lag + step, lag + step)
                pop(group * GROUP + step, step)

        pl.loop(0, free)(contract_group)

        @pl.loop(free, rows // GROUP - 1)
        def block(group):
            for chunk in range(per):
                arrive(group * per + chunk + 1)
            contract_group(group)

        for chunk in range(CHUNKS - GROUP // CHUNK + 1, CHUNKS):
            arrive(chunk)
        for at in range(rows - GROUP, rows):
            if at + lag < rows:
                push(at + lag, at + lag)
            pop(at, at)

    pl.run_scoped(contract, *[pltpu.ACC(at % 2)((2 * RANK, 256), jnp.float32) for at in range(4)])
    term_ref[...] = jnp.zeros_like(term_ref)
    term_ref[:, :, 0:RANK] = jnp.sum(sums_ref[...].reshape(8, 8, RANK, wide), axis=3)


def gradient_kernel(packed_ref, first_ref, terms_ref, gradient_ref):
    packed = packed_ref[...]
    is_third = iota(packed.shape, 0) % 3 == 2

    def gram(block):
        parts = jnp.concatenate(split(block), axis=1)
        whole = lax.dot_general(parts, parts, (((0,), (0,)), ((), ())), preferred_element_type=jnp.float32)
        wide = block.shape[1]
        whole = whole[0:wide] + whole[wide : 2 * wide]
        whole = whole[:, 0:wide] + whole[:, wide : 2 * wide]
        spans = [slice(at, at + RANK) for at in range(0, wide, RANK)]
        return sum(whole[span, span] for span in spans)

    both = gram(jnp.where(is_third, 0.0, packed)) * gram(jnp.where(is_third, packed, 0.0))
    product = jnp.sum(terms_ref[:, :, 0:RANK], axis=0)
    gradient_ref[...] = jnp.dot(first_ref[...], both, precision=HIGHEST) - product


def inhbm(value):
    return pltpu.with_memory_space_constraint(value, pltpu.HBM)


VMEM = pl.BlockSpec(memory_space=pltpu.VMEM)


def on_device(tensor, first, second, third):
    rows, js, ks = tensor.shape
    tensor = inhbm(tensor)
    own, held = pl.pallas_call(
        own_kernel,
        out_shape=(jax.ShapeDtypeStruct((128, 1, 384), jnp.float32), jax.ShapeDtypeStruct(tensor.shape, jnp.float32)),
        in_specs=[pl.BlockSpec(memory_space=pltpu.HBM)] * 3,
        out_specs=(VMEM, VMEM),
        scratch_shapes=[pltpu.VMEM((8, RANK), jnp.float32), pltpu.VMEM((4, RANK), jnp.float32), pltpu.SemaphoreType.DMA((2 + CHUNKS,))],
        compiler_params=pltpu.CompilerParams(vmem_limit_bytes=24 * 1024 * 1024),
        name="own",
    )(inhbm(second), inhbm(third), tensor)
    packed = lax.all_to_all(own, EVERY, 0, 0, tiled=True).reshape(384, 128)
    term, _ = pl.pallas_call(
        term_kernel,
        out_shape=(jax.ShapeDtypeStruct((8, 8, 4 * RANK), jnp.float32), jax.ShapeDtypeStruct(tensor.shape, jnp.float32)),
        in_specs=[pl.BlockSpec(memory_space=pltpu.HBM), VMEM, VMEM],
        out_specs=(VMEM, VMEM),
        input_output_aliases={2: 1},
        scratch_shapes=[
            pltpu.VMEM((ks, 4 * RANK), jnp.float32),
            pltpu.VMEM((js, 4 * RANK), jnp.float32),
            pltpu.VMEM((2 * RANK, ks), jnp.float32),
            pltpu.VMEM((rows, RANK, 4 * RANK), jnp.float32),
            pltpu.SemaphoreType.DMA((CHUNKS,)),
        ],
        compiler_params=pltpu.CompilerParams(vmem_limit_bytes=24 * 1024 * 1024),
        cost_estimate=pl.CostEstimate(flops=2 * rows * js * ks * 512, bytes_accessed=rows * js * ks * 4, transcendentals=0),
        name="term",
    )(tensor, packed, held)
    terms = lax.all_to_all(term, ("ja", "ka"), 0, 0, tiled=True)
    return pl.pallas_call(
        gradient_kernel,
        out_shape=jax.ShapeDtypeStruct(first.shape, jnp.float32),
        in_specs=[VMEM] * 3,
        out_specs=VMEM,
        compiler_params=pltpu.CompilerParams(vmem_limit_bytes=8 * 1024 * 1024),
        name="gradient",
    )(packed, first, terms)


def solution(mesh):
    return jax.shard_map(
        on_device,
        mesh=mesh,
        in_specs=(
            P("ia", "ja", "ka"),
            P(("ia", "ja", "ka"), None),
            P(("ja", "ia", "ka"), None),
            P(("ka", "ia", "ja"), None),
        ),
        out_specs=P(("ia", "ja", "ka"), None),
        check_vma=False,
    )
```

time: 38.6 us -> 35.9 us (0.930)
  blocking collectives: 19.4 us -> 25.8 us
  starting transfers between devices: 3.95 us -> 0 us
  waiting for transfers between devices: 3.46 us -> 0 us
  Pallas kernels: 11.6 us -> 9.72 us
    all_to_all x1 -> x2, blocking collectives: 19.4 us -> 25.8 us  [the longest x1 18 us: on_device(): packed = lax.all_to_all(own, EVERY, 0, 0, tiled=True).reshape(384, 128)]
    all_to_all x1 -> x0, starting transfers between devices: 3.95 us -> none  [on_device(): terms = lax.all_to_all(term, ('ja', 'ka'), 0, 0, tiled=True)]
    all_to_all x1 -> x0, waiting for transfers between devices: 3.46 us -> none  [on_device(): terms = lax.all_to_all(term, ('ja', 'ka'), 0, 0, tiled=True)]
    pallas_call x1, Pallas kernels: 6.02 us -> 3.75 us  [on_device(): pl.pallas_call(term_kernel, out_shape=(jax.ShapeDtypeStruct((8, 8, 4 * RA...]
    pallas_call x1 -> x0, Pallas kernels: 1.27 us -> none  [on_device(): pl.pallas_call(gram_kernel, out_shape=jax.ShapeDtypeStruct(first.shape, j...]
    pallas_call x1, Pallas kernels: 3.59 us -> 4.78 us  [on_device(): pl.pallas_call(own_kernel, out_shape=(jax.ShapeDtypeStruct((128, 1, 384),...]
    pallas_call x1, Pallas kernels: 0.67 us -> 1.19 us  [on_device(): pl.pallas_call(gradient_kernel, out_shape=jax.ShapeDtypeStruct(first.shap...]
  transfers between devices with their start and end apart: 1 -> 0, of which waited for: 1 -> 0; matrix products, arithmetic and copies ran while one was open for 0% -> 0% of each run, Pallas kernels for 3% -> 0%
where the time goes in v3:
time: 35.9 us; the launch traced here: 35.5 us
  blocking collectives  25.8 us (72%)
  Pallas kernels  9.72 us (27%)
    all_to_all x1, blocking collectives, on_device(): packed = lax.all_to_all(own, EVERY, 0, 0, tiled=True).reshape(384, 128)  18 us
    all_to_all x1, blocking collectives, on_device(): terms = lax.all_to_all(term, ('ja', 'ka'), 0, 0, tiled=True)  7.79 us
    pallas_call x1, Pallas kernels, on_device(): pl.pallas_call(own_kernel, out_shape=(jax.ShapeDtypeStruct((128, 1, 384),...  4.78 us
    pallas_call x1, Pallas kernels, on_device(): pl.pallas_call(term_kernel, out_shape=(jax.ShapeDtypeStruct((8, 8, 4 * RA...  3.75 us
    pallas_call x1, Pallas kernels, on_device(): pl.pallas_call(gradient_kernel, out_shape=jax.ShapeDtypeStruct(first.shap...  1.19 us

profile of v3, /device:TPU:1, one launch (start us, length us, event | category | flops | bytes accessed | tf_op | source)
XLA Modules:
  0.0 35.5 jit_solution(9972865714931309628)
XLA Ops:
  0.0 4.8 %own.1 = (f32[128,1,384]{2,1,0:T(1,128)S(1)}, f32[64,256,256]{2,1,0:T(8,128)S(1)}) custom-call(f32[8,32]{1,0:T(8,128)} %second_hbm.1, f32[4,32]{1,0:T(4,128)} %third_hbm.1, f32[64,256,256]{2,1,0:T(8,128)} %tensor_hbm.3), custom_call_target="tpu_custom_call" | custom-call | tf_op jit(solution)/shard_map/own/pallas_call | solution.py:178
  4.8 18.0 %all_to_all.10 = f32[128,1,384]{2,1,0:T(1,128)S(1)} all-to-all(f32[128,1,384]{2,1,0:T(1,128)S(1)} %get-tuple-element.8), channel_id=1, replica_groups=mesh['ia'=16,'ja'=4,'ka'=2] {'ia','ja','ka'}, dimensions={0} | all-to-all | bytes 393216 | tf_op jit(solution)/shard_map/all_to_all | solution.py:187
  22.8 0.0 copy-start
  22.8 3.7 %term.1 = (f32[8,8,128]{2,1,0:T(8,128)S(1)}, f32[64,256,256]{2,1,0:T(8,128)S(1)}) custom-call(f32[64,256,256]{2,1,0:T(8,128)} %tensor_hbm.3, f32[384,128]{1,0:T(8,128)S(1)} %bitcast.1, f32[64,256,256]{2,1,0:T(8,128)S(1)} %get-tuple-element.9.held_ref), custom_call_target="tpu_custom_call", output_to_operand_aliasing={{1}: (2, {})} | custom-call | flops 4294967296 | bytes 16777216 | tf_op jit(solution)/shard_map/term/pallas_call | solution.py:188
  26.5 7.8 %all_to_all.11.terms_ref = f32[8,8,128]{2,1,0:T(8,128)S(1)} all-to-all(f32[8,8,128]{2,1,0:T(8,128)S(1)} %get-tuple-element.10), channel_id=1, replica_groups=mesh['ia'=16,'ja'=4,'ka'=2] {'ja','ka'}, dimensions={0} | all-to-all | bytes 65536 | tf_op jit(solution)/shard_map/all_to_all | solution.py:205
  34.3 0.0 copy-done
  34.3 1.2 %gradient.1 = f32[8,32]{1,0:T(8,128)} custom-call(f32[384,128]{1,0:T(8,128)S(1)} %bitcast.2, f32[8,32]{1,0:T(8,128)S(1)} %copy-done, f32[8,8,128]{2,1,0:T(8,128)S(1)} %all_to_all.11.terms_ref), custom_call_target="tpu_custom_call" | custom-call | tf_op jit(solution)/shard_map/gradient/pallas_call | solution.py:206
Async XLA Ops:
  22.8 11.5 %copy-start = (f32[8,32]{1,0:T(8,128)S(1)}, f32[8,32]{1,0:T(8,128)}, u32[]{:S(2)}) copy-start(f32[8,32]{1,0:T(8,128)} %first_ref.1) | copy-start | bytes 3076

commit v4 on v3

--- a/solution.py
+++ b/solution.py
@@ -51,12 +51,7 @@
         chunk_copy(tensor_hbm, tensor_ref, sems.at[2 + at], at).start()
 
     def row(value):
-        count = value.shape[0]
-        lanes = count * RANK
-        spread = jnp.where(iota((RANK, lanes), 0) == iota((RANK, lanes), 1) % RANK, 1.0, 0.0)
-        wide = jnp.dot(value, spread, precision=HIGHEST)
-        kept = jnp.where(iota((count, lanes), 1) // RANK == iota((count, lanes), 0), wide, 0.0)
-        return jnp.sum(kept, axis=0, keepdims=True)
+        return jnp.concatenate([value[at : at + 1] for at in range(value.shape[0])], axis=1)
 
     second_copy.wait()
     third_copy.wait()

time: 35.9 us -> 35.8 us (level)
  no operation moved by 1% of the time
where the time goes in v4:
time: 35.8 us; the launch traced here: 35.4 us
  blocking collectives  25.7 us (72%)
  Pallas kernels  9.72 us (27%)
    all_to_all x1, blocking collectives, on_device(): packed = lax.all_to_all(own, EVERY, 0, 0, tiled=True).reshape(384, 128)  17.9 us
    all_to_all x1, blocking collectives, on_device(): terms = lax.all_to_all(term, ('ja', 'ka'), 0, 0, tiled=True)  7.8 us
    pallas_call x1, Pallas kernels, on_device(): pl.pallas_call(own_kernel, out_shape=(jax.ShapeDtypeStruct((128, 1, 384),...  4.78 us
    pallas_call x1, Pallas kernels, on_device(): pl.pallas_call(term_kernel, out_shape=(jax.ShapeDtypeStruct((8, 8, 4 * RA...  3.74 us
    pallas_call x1, Pallas kernels, on_device(): pl.pallas_call(gradient_kernel, out_shape=jax.ShapeDtypeStruct(first.shap...  1.19 us

profile of v4, /device:TPU:1, one launch (start us, length us, event | category | flops | bytes accessed | tf_op | source)
XLA Modules:
  0.0 35.4 jit_solution(245061491016729111)
XLA Ops:
  0.0 4.8 %own.1 = (f32[128,1,384]{2,1,0:T(1,128)S(1)}, f32[64,256,256]{2,1,0:T(8,128)S(1)}) custom-call(f32[8,32]{1,0:T(8,128)} %second_hbm.1, f32[4,32]{1,0:T(4,128)} %third_hbm.1, f32[64,256,256]{2,1,0:T(8,128)} %tensor_hbm.3), custom_call_target="tpu_custom_call" | custom-call | tf_op jit(solution)/shard_map/own/pallas_call | solution.py:173
  4.8 17.9 %all_to_all.10 = f32[128,1,384]{2,1,0:T(1,128)S(1)} all-to-all(f32[128,1,384]{2,1,0:T(1,128)S(1)} %get-tuple-element.8), channel_id=1, replica_groups=mesh['ia'=16,'ja'=4,'ka'=2] {'ia','ja','ka'}, dimensions={0} | all-to-all | bytes 393216 | tf_op jit(solution)/shard_map/all_to_all | solution.py:182
  22.7 0.0 copy-start
  22.7 3.7 %term.1 = (f32[8,8,128]{2,1,0:T(8,128)S(1)}, f32[64,256,256]{2,1,0:T(8,128)S(1)}) custom-call(f32[64,256,256]{2,1,0:T(8,128)} %tensor_hbm.3, f32[384,128]{1,0:T(8,128)S(1)} %bitcast.1, f32[64,256,256]{2,1,0:T(8,128)S(1)} %get-tuple-element.9.held_ref), custom_call_target="tpu_custom_call", output_to_operand_aliasing={{1}: (2, {})} | custom-call | flops 4294967296 | bytes 16777216 | tf_op jit(solution)/shard_map/term/pallas_call | solution.py:183
  26.5 7.8 %all_to_all.11.terms_ref = f32[8,8,128]{2,1,0:T(8,128)S(1)} all-to-all(f32[8,8,128]{2,1,0:T(8,128)S(1)} %get-tuple-element.10), channel_id=1, replica_groups=mesh['ia'=16,'ja'=4,'ka'=2] {'ja','ka'}, dimensions={0} | all-to-all | bytes 65536 | tf_op jit(solution)/shard_map/all_to_all | solution.py:200
  34.3 0.0 copy-done
  34.3 1.2 %gradient.1 = f32[8,32]{1,0:T(8,128)} custom-call(f32[384,128]{1,0:T(8,128)S(1)} %bitcast.2, f32[8,32]{1,0:T(8,128)S(1)} %copy-done, f32[8,8,128]{2,1,0:T(8,128)S(1)} %all_to_all.11.terms_ref), custom_call_target="tpu_custom_call" | custom-call | tf_op jit(solution)/shard_map/gradient/pallas_call | solution.py:201
Async XLA Ops:
  22.7 11.6 %copy-start = (f32[8,32]{1,0:T(8,128)S(1)}, f32[8,32]{1,0:T(8,128)}, u32[]{:S(2)}) copy-start(f32[8,32]{1,0:T(8,128)} %first_ref.1) | copy-start | bytes 3076
